TPU v7x, 32 devices: a whole 2x2x4 slice. The times are simulated.
32 devices in a mesh: rows: 8 (over z, y), groups: 4 (over x, core).
Axes of the slice: x: 2, y: 2, z: 4, core: 2. Of those that a mesh axis runs over, the one named last changes fastest.
Arguments:
- snapshots: bfloat16 [16384, 1024], P('rows', 'groups'), may hold values from -6 to 6
- mass_diag: float32 [16384], P('rows'), may hold values from 0.5 to 2
- lower_coupling: float32 [8, 128, 128], P('rows'), may hold values from -0.5 to 0.5
- upper_coupling: float32 [8, 128, 128], P('rows'), may hold values from -0.5 to 0.5
- band_offsets: int32 [8, 2], P('rows'), may hold values from 1 to 2
- start_basis: float32 [1024, 512], replicated, may hold values from -6 to 6
Outputs:
- modes: float32 [16384, 512], P('rows', 'groups')
All inputs are finite; a program needn't handle non-finite values.
Results may differ from a plain program's by a relative error of at most 0.0042.
Values may be sent and summed in bfloat16 or wider, within the bound.
A program may use at most 128 MiB of HBM per device.

v0:
```python
import jax
import jax.numpy as jnp
from jax import lax
from jax.sharding import PartitionSpec as P

ITERS = 3


def from_behind(value, axis, by):
    devices = lax.axis_size(axis)
    pairs = [(i, i + by) for i in range(devices) if 0 <= i + by < devices]
    return lax.ppermute(value, axis, pairs)


def orthonormal(image):
    correlation = jnp.dot(
        image.T, image, precision=lax.Precision.HIGHEST, preferred_element_type=jnp.float32
    )
    lower = jnp.linalg.cholesky(correlation)
    return lax.linalg.triangular_solve(lower, image, left_side=False, lower=True, transpose_a=True)


def pass_down(piece):
    return from_behind(piece, "rows", 1)


def pass_up(piece):
    return from_behind(piece, "rows", -1)


def shards(snapshots, mass_diag, lower_coupling, upper_coupling, band_offsets, start_basis):
    block_rows = snapshots.shape[0]
    rim_rows = lower_coupling.shape[1]
    total_rows = block_rows * lax.axis_size("rows")
    bottom_rim = snapshots[block_rows - rim_rows :, :]
    top_rim = snapshots[:rim_rows, :]
    below_one = pass_down(bottom_rim)
    below_two = pass_down(below_one)
    above_one = pass_up(top_rim)
    above_two = pass_up(above_one)
    lower_rims = jnp.where(band_offsets[0, 0] == 1, below_one, below_two).astype(jnp.float32)
    upper_rims = jnp.where(band_offsets[0, 1] == 1, above_one, above_two).astype(jnp.float32)
    lower_terms = jnp.dot(
        lower_coupling[0],
        lower_rims,
        precision=lax.Precision.HIGHEST,
        preferred_element_type=jnp.float32,
    )
    upper_terms = jnp.dot(
        upper_coupling[0],
        upper_rims,
        precision=lax.Precision.HIGHEST,
        preferred_element_type=jnp.float32,
    )
    weighted = mass_diag[:, None] * snapshots.astype(jnp.float32)
    weighted = weighted.at[:rim_rows, :].add(lower_terms)
    weighted = weighted.at[block_rows - rim_rows :, :].add(upper_terms)
    weighted = weighted.astype(jnp.bfloat16)
    gathered = lax.all_gather(weighted, "groups", axis=1, tiled=True)
    gram_cols = lax.dot_general(
        gathered, weighted, (((0,), (0,)), ((), ())), preferred_element_type=jnp.float32
    )
    gram_cols = lax.psum(gram_cols, "rows") / total_rows
    basis = start_basis
    gram = lax.all_gather(gram_cols, "groups", axis=1, tiled=True)
    for turn_index in range(ITERS):
        image = jnp.dot(
            gram, basis, precision=lax.Precision.HIGHEST, preferred_element_type=jnp.float32
        )
        basis = orthonormal(image)
    basis_low = basis.astype(jnp.bfloat16)
    group_index = lax.axis_index("groups")
    mode_cols = basis_low.shape[1] // lax.axis_size("groups")
    basis_part = lax.dynamic_slice_in_dim(basis_low, group_index * mode_cols, mode_cols, 1)
    return jnp.dot(gathered, basis_part, preferred_element_type=jnp.float32)


def solution(mesh):
    placed = (
        P("rows", "groups"),
        P("rows"),
        P("rows", None, None),
        P("rows", None, None),
        P("rows", None),
        P(),
    )
    return jax.shard_map(
        shards, mesh=mesh, in_specs=placed, out_specs=P("rows", "groups"), check_vma=False
    )
```

profile of v0, /device:TPU:0, one launch (start us, length us, event | category | flops | bytes accessed | tf_op | source)
XLA Modules:
  0.0 700.9 jit_solution(16305308095605062142)
XLA Ops:
  30.0 36.2 %all-gather.3.cloned.1.call-done = bf16[2048,1024]{0,1:T(8,128)(2,1)} async-done(((bf16[2048,256]{0,1:T(8,128)(2,1)}), bf16[2048,1024]{0,1:T(8,128)(2,1)}) %all-gather.3.cloned.1.call-update) | async-done | bytes 4194320 | tf_op jit(solution)/shard_map/all_gather | solution.py:59
  71.1 78.1 %all-reduce.3.cloned.1.call-done = f32[1024,256]{1,0:T(8,128)} async-done(((f32[1024,256]{1,0:T(8,128)}), f32[1024,256]{1,0:T(8,128)}) %all-reduce.3.cloned.1.call-update) | async-done | bytes 1048592 | tf_op jit(solution)/shard_map/psum | solution.py:63
  151.5 34.2 %all-gather.5.cloned.1.call-done = f32[1024,1024]{1,0:T(8,128)} async-done(((f32[1024,256]{1,0:T(8,128)}), f32[1024,1024]{1,0:T(8,128)}) %all-gather.5.cloned.1.call-update) | async-done | bytes 4194320 | tf_op jit(solution)/shard_map/all_gather | solution.py:65
  185.7 8.8 %fusion.160 = f32[1024,512]{1,0:T(8,128)S(1)} fusion(f32[1024,1024]{1,0:T(8,128)} %all-gather.5.cloned.1.call-done, f32[1024,512]{1,0:T(8,128)S(1)} %copy-done), kind=kOutput, calls=%fused_computation.247 | convolution fusion | flops 6442450944 | bytes 8388608 | tf_op jit(solution)/shard_map/dot_general | solution.py:67
  203.3 11.7 %cholesky.374 = f32[128,128]{1,0:T(8,128)S(1)} custom-call(f32[128,128]{1,0:T(8,128)S(1)} %cholesky.586), custom_call_target="Cholesky" | custom-call | tf_op jit(solution)/shard_map/jit(cholesky)/cholesky | solution.py:19
  215.1 9.8 %custom-call.31 = f32[1,128,128]{1,2,0:T(8,128)S(1)} custom-call(f32[1,128,128]{2,1,0:T(8,128)S(1)} %get-tuple-element.115), custom_call_target="InvertDiagBlocksLowerTriangular" | custom-call | tf_op jit(solution)/shard_map/jit(cholesky)/cholesky | solution.py:19
  227.5 12.1 %cholesky.393 = f32[128,128]{1,0:T(8,128)S(1)} custom-call(f32[128,128]{1,0:T(8,128)S(1)} %cholesky.590), custom_call_target="Cholesky" | custom-call | tf_op jit(solution)/shard_map/jit(cholesky)/cholesky | solution.py:19
  239.7 9.8 %custom-call.32 = f32[1,128,128]{1,2,0:T(8,128)S(1)} custom-call(f32[1,128,128]{2,1,0:T(8,128)S(1)} %get-tuple-element.112), custom_call_target="InvertDiagBlocksLowerTriangular" | custom-call | tf_op jit(solution)/shard_map/jit(cholesky)/cholesky | solution.py:19
  251.1 11.7 %cholesky.414 = f32[128,128]{1,0:T(8,128)S(1)} custom-call(f32[128,128]{1,0:T(8,128)S(1)} %cholesky.595), custom_call_target="Cholesky" | custom-call | tf_op jit(solution)/shard_map/jit(cholesky)/cholesky | solution.py:19
  263.5 9.8 %custom-call.33 = f32[1,128,128]{1,2,0:T(8,128)S(1)} custom-call(f32[1,128,128]{2,1,0:T(8,128)S(1)} %get-tuple-element.109), custom_call_target="InvertDiagBlocksLowerTriangular" | custom-call | tf_op jit(solution)/shard_map/jit(cholesky)/cholesky | solution.py:19
  274.7 11.9 %cholesky.431 = f32[128,128]{1,0:T(8,128)S(1)} custom-call(f32[128,128]{1,0:T(8,128)S(1)} %convolution_subtract_fusion.14), custom_call_target="Cholesky" | custom-call | tf_op jit(solution)/shard_map/jit(cholesky)/cholesky | solution.py:19
  291.5 11.5 %while.8 = (s32[]{:T(128)}, f32[512,512]{1,0:T(8,128)}, s32[4,2]{0,1:T(2,128)S(1)}, f32[4,128,128]{2,1,0:T(8,128)S(1)}, s32[]{:T(128)}) while((s32[]{:T(128)}, f32[512,512]{1,0:T(8,128)}, s32[4,2]{0,1:T(2,128)S(1)}, f32[4,128,128]{2,1,0:T(8,128)S(1)}, s32[]{:T(128)}) %tuple.82), condition=%wide.while_cond.2, body=%wide.while_body.2.sunk | while | flops 2 | bytes 131181 | solution.py:20
  303.0 39.3 %custom-call.34 = f32[4,128,128]{1,2,0:T(8,128)S(1)} custom-call(f32[4,128,128]{2,1,0:T(8,128)S(1)} %get-tuple-element.51), custom_call_target="InvertDiagBlocksLowerTriangular" | custom-call | tf_op jit(solution)/shard_map/triangular_solve/custom-call.3 | solution.py:20
  354.9 7.1 %fusion = f32[1024,512]{1,0:T(8,128)S(1)} fusion(f32[1024,1024]{1,0:T(8,128)S(1)} %copy-done.1, f32[1024,128]{0,1:T(8,128)S(1)} %fusion.107, f32[1024,128]{0,1:T(8,128)S(1)} %fusion.108, f32[1024,128]{0,1:T(8,128)S(1)} %fusion.109, f32[1024,128]{0,1:T(8,128)S(1)} %bitcast.188), kind=kOutput, calls=%fused_computation.6 | convolution fusion | flops 6444023808 | bytes 8388608 | tf_op jit(solution)/shard_map/dot_general | solution.py:67
  370.9 11.7 %cholesky.446 = f32[128,128]{1,0:T(8,128)S(1)} custom-call(f32[128,128]{1,0:T(8,128)S(1)} %cholesky.599), custom_call_target="Cholesky" | custom-call | tf_op jit(solution)/shard_map/jit(cholesky)/cholesky | solution.py:19
  382.8 9.9 %custom-call.35 = f32[1,128,128]{1,2,0:T(8,128)S(1)} custom-call(f32[1,128,128]{2,1,0:T(8,128)S(1)} %get-tuple-element.105), custom_call_target="InvertDiagBlocksLowerTriangular" | custom-call | tf_op jit(solution)/shard_map/jit(cholesky)/cholesky | solution.py:19
  395.2 11.7 %cholesky.465 = f32[128,128]{1,0:T(8,128)S(1)} custom-call(f32[128,128]{1,0:T(8,128)S(1)} %cholesky.603), custom_call_target="Cholesky" | custom-call | tf_op jit(solution)/shard_map/jit(cholesky)/cholesky | solution.py:19
  408.4 9.8 %custom-call.36 = f32[1,128,128]{1,2,0:T(8,128)S(1)} custom-call(f32[1,128,128]{2,1,0:T(8,128)S(1)} %get-tuple-element.102), custom_call_target="InvertDiagBlocksLowerTriangular" | custom-call | tf_op jit(solution)/shard_map/jit(cholesky)/cholesky | solution.py:19
  419.8 11.7 %cholesky.486 = f32[128,128]{1,0:T(8,128)S(1)} custom-call(f32[128,128]{1,0:T(8,128)S(1)} %cholesky.608), custom_call_target="Cholesky" | custom-call | tf_op jit(solution)/shard_map/jit(cholesky)/cholesky | solution.py:19
  432.2 10.0 %custom-call.37 = f32[1,128,128]{1,2,0:T(8,128)S(1)} custom-call(f32[1,128,128]{2,1,0:T(8,128)S(1)} %get-tuple-element.99), custom_call_target="InvertDiagBlocksLowerTriangular" | custom-call | tf_op jit(solution)/shard_map/jit(cholesky)/cholesky | solution.py:19
  443.6 11.7 %cholesky.503 = f32[128,128]{1,0:T(8,128)S(1)} custom-call(f32[128,128]{1,0:T(8,128)S(1)} %convolution_subtract_fusion.13), custom_call_target="Cholesky" | custom-call | tf_op jit(solution)/shard_map/jit(cholesky)/cholesky | solution.py:19
  459.7 11.8 %while.9 = (s32[]{:T(128)}, f32[512,512]{1,0:T(8,128)}, s32[4,2]{0,1:T(2,128)S(1)}, f32[4,128,128]{2,1,0:T(8,128)S(1)}, s32[]{:T(128)}) while((s32[]{:T(128)}, f32[512,512]{1,0:T(8,128)}, s32[4,2]{0,1:T(2,128)S(1)}, f32[4,128,128]{2,1,0:T(8,128)S(1)}, s32[]{:T(128)}) %tuple.97), condition=%wide.while_cond.2.clone, body=%wide.while_body.2.clone.sunk | while | flops 2 | bytes 131181 | solution.py:20
  471.4 39.7 %custom-call.38 = f32[4,128,128]{1,2,0:T(8,128)S(1)} custom-call(f32[4,128,128]{2,1,0:T(8,128)S(1)} %get-tuple-element.52), custom_call_target="InvertDiagBlocksLowerTriangular" | custom-call | tf_op jit(solution)/shard_map/triangular_solve/custom-call.3 | solution.py:20
  539.4 11.7 %cholesky.518 = f32[128,128]{1,0:T(8,128)S(1)} custom-call(f32[128,128]{1,0:T(8,128)S(1)} %cholesky.612), custom_call_target="Cholesky" | custom-call | tf_op jit(solution)/shard_map/jit(cholesky)/cholesky | solution.py:19
  551.3 10.0 %custom-call.39 = f32[1,128,128]{1,2,0:T(8,128)S(1)} custom-call(f32[1,128,128]{2,1,0:T(8,128)S(1)} %get-tuple-element.95), custom_call_target="InvertDiagBlocksLowerTriangular" | custom-call | tf_op jit(solution)/shard_map/jit(cholesky)/cholesky | solution.py:19
  563.8 11.7 %cholesky.537 = f32[128,128]{1,0:T(8,128)S(1)} custom-call(f32[128,128]{1,0:T(8,128)S(1)} %cholesky.616), custom_call_target="Cholesky" | custom-call | tf_op jit(solution)/shard_map/jit(cholesky)/cholesky | solution.py:19
  576.9 9.8 %custom-call.40 = f32[1,128,128]{1,2,0:T(8,128)S(1)} custom-call(f32[1,128,128]{2,1,0:T(8,128)S(1)} %get-tuple-element.92), custom_call_target="InvertDiagBlocksLowerTriangular" | custom-call | tf_op jit(solution)/shard_map/jit(cholesky)/cholesky | solution.py:19
  588.2 11.7 %cholesky.558 = f32[128,128]{1,0:T(8,128)S(1)} custom-call(f32[128,128]{1,0:T(8,128)S(1)} %cholesky.621), custom_call_target="Cholesky" | custom-call | tf_op jit(solution)/shard_map/jit(cholesky)/cholesky | solution.py:19
  600.7 10.2 %custom-call.41 = f32[1,128,128]{1,2,0:T(8,128)S(1)} custom-call(f32[1,128,128]{2,1,0:T(8,128)S(1)} %get-tuple-element.89), custom_call_target="InvertDiagBlocksLowerTriangular" | custom-call | tf_op jit(solution)/shard_map/jit(cholesky)/cholesky | solution.py:19
  612.3 11.7 %cholesky.575 = f32[128,128]{1,0:T(8,128)S(1)} custom-call(f32[128,128]{1,0:T(8,128)S(1)} %convolution_subtract_fusion.12), custom_call_target="Cholesky" | custom-call | tf_op jit(solution)/shard_map/jit(cholesky)/cholesky | solution.py:19
  628.3 11.3 %while.10 = (s32[]{:T(128)}, f32[512,512]{1,0:T(8,128)}, s32[4,2]{0,1:T(2,128)S(1)}, f32[4,128,128]{2,1,0:T(8,128)S(1)}, s32[]{:T(128)}) while((s32[]{:T(128)}, f32[512,512]{1,0:T(8,128)}, s32[4,2]{0,1:T(2,128)S(1)}, f32[4,128,128]{2,1,0:T(8,128)S(1)}, s32[]{:T(128)}) %tuple.98), condition=%wide.while_cond.2.clone.1, body=%wide.while_body.2.clone.1.sunk | while | flops 2 | bytes 131181 | solution.py:20
  639.7 39.5 %custom-call.42 = f32[4,128,128]{1,2,0:T(8,128)S(1)} custom-call(f32[4,128,128]{2,1,0:T(8,128)S(1)} %get-tuple-element.53), custom_call_target="InvertDiagBlocksLowerTriangular" | custom-call | tf_op jit(solution)/shard_map/triangular_solve/custom-call.3 | solution.py:20
  (186 shorter events, 164.6 us)
Async XLA Ops:
  6.5 179.2 %copy-start = (f32[1024,512]{1,0:T(8,128)S(1)}, f32[1024,512]{1,0:T(8,128)}, u32[]{:S(2)}) copy-start(f32[1024,512]{1,0:T(8,128)} %param.18) | copy-start | bytes 6291460
  6.5 8.7 %copy-start.15 = (f32[2048]{0:T(1024)S(1)}, f32[2048]{0:T(1024)}, u32[]{:S(2)}) copy-start(f32[2048]{0:T(1024)} %param.14) | copy-start | bytes 24580
  6.5 59.7 %all-gather.3.cloned.1.call-start = ((), (), s32[]{:S(2)}) async-start(), calls=%async_computation | async-start | bytes 5242880 | tf_op jit(solution)/shard_map/all_gather | solution.py:59
  7.6 8.0 %collective-permute-start = (bf16[128,256]{1,0:T(8,128)(2,1)S(1)}, bf16[128,256]{1,0:T(8,128)(2,1)S(1)}, u32[]{:S(2)}, u32[]{:S(2)}) collective-permute-start(bf16[128,256]{1,0:T(8,128)(2,1)S(1)} %get-tuple-element.85), channel_id=1, source_target_pairs={{0,4},{4,8},{8,12},{12,16},{16,20},{20,24},{24,28},{1,5},{5,9},{9,... | collective-permute-start | bytes 196616 | tf_op jit(solution)/shard_map/ppermute | solution.py:12
  12.5 9.5 %collective-permute-start.2 = (bf16[128,256]{1,0:T(8,128)(2,1)S(1)}, bf16[128,256]{1,0:T(8,128)(2,1)S(1)}, u32[]{:S(2)}, u32[]{:S(2)}) collective-permute-start(bf16[128,256]{1,0:T(8,128)(2,1)S(1)} %get-tuple-element.84), channel_id=1, source_target_pairs={{4,0},{8,4},{12,8},{16,12},{20,16},{24,20},{28,24},{5,1},{9,5},{13... | collective-permute-start | bytes 196616 | tf_op jit(solution)/shard_map/ppermute | solution.py:12
  15.3 4.9 copy-start.16
  15.3 8.0 %copy-start.13 = (f32[1,128,128]{2,1,0:T(8,128)S(1)}, f32[1,128,128]{2,1,0:T(8,128)}, u32[]{:S(2)}) copy-start(f32[1,128,128]{2,1,0:T(8,128)} %param.15) | copy-start | bytes 196612
  15.3 13.2 %copy-start.14 = (f32[1,128,128]{2,1,0:T(8,128)S(1)}, f32[1,128,128]{2,1,0:T(8,128)}, u32[]{:S(2)}) copy-start(f32[1,128,128]{2,1,0:T(8,128)} %param.16) | copy-start | bytes 196612
  15.6 7.7 %collective-permute-start.1 = (bf16[128,256]{1,0:T(8,128)(2,1)S(1)}, bf16[128,256]{1,0:T(8,128)(2,1)S(1)}, u32[]{:S(2)}, u32[]{:S(2)}) collective-permute-start(bf16[128,256]{1,0:T(8,128)(2,1)S(1)} %collective-permute-done), channel_id=1, source_target_pairs={{0,4},{4,8},{8,12},{12,16},{16,20},{20,24},{24,28},{1,5},{5,9},{9,... | collective-permute-start | bytes 196616 | tf_op jit(solution)/shard_map/ppermute | solution.py:12
  22.0 6.6 collective-permute-start.3
  30.0 119.2 %all-reduce.3.cloned.1.call-start = ((), (), s32[]{:S(2)}) async-start(), calls=%async_computation.1 | async-start | bytes 2097152 | tf_op jit(solution)/shard_map/psum | solution.py:63
  71.1 114.7 %all-gather.5.cloned.1.call-start = ((), (), s32[]{:S(2)}) async-start(), calls=%async_computation.2 | async-start | bytes 5242880 | tf_op jit(solution)/shard_map/all_gather | solution.py:65
  194.5 1.4 copy-start.7
  202.3 1.0 copy-start.12
  342.3 4.6 copy-start.8
  349.7 5.2 copy-start.1
  362.1 1.4 copy-start.5
  369.9 1.0 copy-start.10
  511.2 4.6 copy-start.6
  518.5 5.2 copy-start.2
  530.7 1.3 copy-start.3
  538.4 1.0 copy-start.11
  679.1 4.6 copy-start.4
  686.5 5.3 copy-start.9
Sparse Core Ops, SparseCore 0:
  30.1 36.0 all-gather.2
  71.2 77.9 all-reduce.2
  151.6 34.0 all-gather.4
where the time goes:
time: 707 us; the launch traced here: 701 us
  other arithmetic  368 us (52%)
  waiting for transfers between devices  154 us (22%)
  matrix products  95.6 us (14%)
  local copies, waits for them, and re-layouts  48.9 us (7%)
  between operations  22.9 us (3%)
  starting transfers between devices  12.1 us (2%)
    another operation x44, other arithmetic, orthonormal(): lower = jnp.linalg.cholesky(correlation)  238 us
    another operation x7, other arithmetic, orthonormal(): lax.linalg.triangular_solve(lower, image, left_side=False, lower=True, tr...  122 us
    psum x1, waiting for transfers between devices, shards(): gram_cols = lax.psum(gram_cols, 'rows') / total_rows  78.1 us
    another operation x21, matrix products, orthonormal(): lax.linalg.triangular_solve(lower, image, left_side=False, lower=True, tr...  37.5 us
    all_gather x1, waiting for transfers between devices, shards(): gathered = lax.all_gather(weighted, 'groups', axis=1, tiled=True)  36.2 us
    another operation x40, local copies, waits for them, and re-layouts, orthonormal(): lax.linalg.triangular_solve(lower, image, left_side=False, lower=True, tr...  34.4 us
    all_gather x1, waiting for transfers between devices, shards(): gram = lax.all_gather(gram_cols, 'groups', axis=1, tiled=True)  34.2 us
    dot_general x3, matrix products, shards(): jnp.dot(gram, basis, precision=lax.Precision.HIGHEST, preferred_element_t...  22.9 us
  transfers between devices with their start and end apart: 7, of which 4 were waited for; matrix products, arithmetic and copies ran while one was open for 0% of the time, Pallas kernels for 0%

commit v1 on v0

v1 whole, which is shorter than its diff:
```python
import functools

import jax
import jax.numpy as jnp
from jax import lax
from jax.experimental import pallas as pl
from jax.experimental.pallas import tpu as pltpu
from jax.sharding import PartitionSpec as P

ITERS = 3
BF16 = jnp.bfloat16
F32 = jnp.float32

LOOSE = 0.04
TIGHT = 0.003
REFINED = 1e-4
MOST_STEPS = 14


def dot_nn(a, b):
    return lax.dot_general(a, b, (((1,), (0,)), ((), ())), preferred_element_type=F32)


def dot_nt(a, b):
    return lax.dot_general(a, b, (((1,), (1,)), ((), ())), preferred_element_type=F32)


def split(value):
    high = value.astype(BF16)
    return high, (value - high.astype(F32)).astype(BF16)


def ids(shape):
    return lax.broadcasted_iota(jnp.int32, shape, 0), lax.broadcasted_iota(jnp.int32, shape, 1)


def half_lower(residual):
    row, col = ids(residual.shape)
    return jnp.where(row > col, residual, jnp.where(row == col, 0.5 * residual, 0.0))


def minus_identity(product):
    row, col = ids(product.shape)
    return product - jnp.where(row == col, 1.0, 0.0)


def triangular_inverse(corr, limit, corr_ref, x_ref):
    modes = corr.shape[0]
    row, col = ids(corr.shape)
    diagonal = jnp.where(row == col, corr, 0.0)
    scale_rows = lax.rsqrt(jnp.sum(diagonal, axis=1, keepdims=True))
    scale_cols = lax.rsqrt(jnp.sum(diagonal, axis=0, keepdims=True))
    scaled = corr * scale_rows * scale_cols
    corr_ref[...] = scaled.astype(BF16)
    x_ref[...] = jnp.where(row > col, -scaled, jnp.where(row == col, 1.0, 0.0)).astype(BF16)

    def more(state):
        return (state[0] < MOST_STEPS) & (state[1] > limit * modes)

    def step(state):
        x = x_ref[...]
        half = dot_nn(x, corr_ref[...]).astype(BF16)
        residual = minus_identity(dot_nt(half, x))
        size = jnp.sum(residual * residual)
        change = dot_nn(half_lower(residual).astype(BF16), x)
        x_ref[...] = (x.astype(F32) - change).astype(BF16)
        return state[0] + 1, size

    _, size = lax.while_loop(more, step, (jnp.int32(0), jnp.float32(jnp.inf)))
    x = x_ref[...].astype(F32)
    smallest = jnp.min(jnp.where(row == col, x, 1.0))
    x_ref[...] = (x * scale_cols).astype(BF16)
    return (size <= limit * modes) & (smallest > 0.0)


def start_kernel(start_ref, high_ref, low_ref, ok_ref, corr_ref, x_ref):
    high, low = split(start_ref[...])
    ok = triangular_inverse(dot_nt(high, high), LOOSE, corr_ref, x_ref)
    x = x_ref[...]
    high_ref[...], low_ref[...] = split(dot_nn(x, high) + dot_nn(x, low))
    ok_ref[0] = ok.astype(jnp.int32)


def iterate_kernel(
    part_ref, gram_ref, high_in, low_in, basis_ref, ok_ref, gram_high, gram_low, image, high, low, corr_ref, x_ref, e_ref
):
    modes, snaps = image.shape
    tile = 256
    part_modes = basis_ref.shape[0]

    def split_gram(step, carry):
        rows = pl.ds(pl.multiple_of(step * tile, tile), tile)
        gram_high[rows, :], gram_low[rows, :] = split(gram_ref[rows, :])
        return carry

    lax.fori_loop(0, snaps // tile, split_gram, 0)
    high[...] = high_in[...]
    low[...] = low_in[...]
    ok = jnp.bool_(True)
    for turn in range(ITERS):

        def multiply(step, carry):
            cols = pl.ds(pl.multiple_of(step * tile, tile), tile)
            g = gram_high[:, cols]
            image[:, cols] = dot_nn(high[...], g) + (dot_nn(high[...], gram_low[:, cols]) + dot_nn(low[...], g))
            return carry

        lax.fori_loop(0, snaps // tile, multiply, 0)
        high[...], low[...] = split(image[...])
        limit = TIGHT if turn == ITERS - 1 else LOOSE
        ok = ok & triangular_inverse(dot_nt(high[...], high[...]), limit, corr_ref, x_ref)

        def apply(step, carry):
            cols = pl.ds(pl.multiple_of(step * tile, tile), tile)
            x = x_ref[...]
            image[:, cols] = dot_nn(x, high[:, cols]) + dot_nn(x, low[:, cols])
            return carry

        lax.fori_loop(0, snaps // tile, apply, 0)
        high[...], low[...] = split(image[...])

    def more(state):
        return (state[0] < 4) & (state[1] > REFINED * modes)

    def refine(state):
        cross = dot_nt(high[...], low[...])
        residual = minus_identity(dot_nt(high[...], high[...]) + (cross + dot_nt(low[...], high[...])))
        size = jnp.sum(residual * residual)
        e_ref[...] = half_lower(residual).astype(BF16)

        @pl.when(size > REFINED * modes)
        def _():
            image[...] = image[...] - dot_nn(e_ref[...], high[...])
            high[...], low[...] = split(image[...])

        return state[0] + 1, size

    _, size = lax.while_loop(more, refine, (jnp.int32(0), jnp.float32(jnp.inf)))
    rows = pl.ds(pl.multiple_of(part_ref[0] * part_modes, part_modes), part_modes)
    basis_ref[...] = (image[rows, :] - dot_nn(e_ref[rows, :], high[...])).astype(BF16)
    ok_ref[0] = (ok & (size <= REFINED * modes)).astype(jnp.int32)


VMEM = pl.BlockSpec(memory_space=pltpu.VMEM)
SMEM = pl.BlockSpec(memory_space=pltpu.SMEM)
LIMIT = 56 * 2**20


def prepare_start(start_basis):
    snaps, modes = start_basis.shape
    return pl.pallas_call(
        start_kernel,
        name="prepare_start",
        out_shape=(
            jax.ShapeDtypeStruct((modes, snaps), BF16),
            jax.ShapeDtypeStruct((modes, snaps), BF16),
            jax.ShapeDtypeStruct((1,), jnp.int32),
        ),
        in_specs=[VMEM],
        out_specs=(VMEM, VMEM, SMEM),
        scratch_shapes=[pltpu.VMEM((modes, modes), BF16), pltpu.VMEM((modes, modes), BF16)],
        compiler_params=pltpu.CompilerParams(vmem_limit_bytes=LIMIT),
        cost_estimate=pl.CostEstimate(flops=30 * modes**3, bytes_accessed=4 * snaps * modes, transcendentals=0),
    )(start_basis.T)


def iterate(part, part_modes, gram, high, low):
    modes, snaps = high.shape
    return pl.pallas_call(
        iterate_kernel,
        name="iterate",
        out_shape=(jax.ShapeDtypeStruct((part_modes, snaps), BF16), jax.ShapeDtypeStruct((1,), jnp.int32)),
        in_specs=[SMEM, VMEM, VMEM, VMEM],
        out_specs=(VMEM, SMEM),
        scratch_shapes=[
            pltpu.VMEM((snaps, snaps), BF16),
            pltpu.VMEM((snaps, snaps), BF16),
            pltpu.VMEM((modes, snaps), F32),
            pltpu.VMEM((modes, snaps), BF16),
            pltpu.VMEM((modes, snaps), BF16),
            pltpu.VMEM((modes, modes), BF16),
            pltpu.VMEM((modes, modes), BF16),
            pltpu.VMEM((modes, modes), BF16),
        ],
        compiler_params=pltpu.CompilerParams(vmem_limit_bytes=LIMIT),
        cost_estimate=pl.CostEstimate(flops=150 * modes**3, bytes_accessed=4 * snaps * snaps, transcendentals=0),
    )(part, gram, high, low)


def orthonormal(image):
    correlation = jnp.dot(image.T, image, precision=lax.Precision.HIGHEST, preferred_element_type=F32)
    lower = jnp.linalg.cholesky(correlation)
    return lax.linalg.triangular_solve(lower, image, left_side=False, lower=True, transpose_a=True)


def direct_part(group_index, part_modes, gram, start_basis):
    basis = start_basis
    for _ in range(ITERS):
        image = jnp.dot(gram, basis, precision=lax.Precision.HIGHEST, preferred_element_type=F32)
        basis = orthonormal(image)
    return lax.dynamic_slice_in_dim(basis.astype(BF16).T, group_index * part_modes, part_modes, 0)


def from_behind(value, axis, by):
    devices = lax.axis_size(axis)
    pairs = [(i, i + by) for i in range(devices) if 0 <= i + by < devices]
    return lax.ppermute(value, axis, pairs)


def rim_terms(coupling, rims):
    return jnp.dot(coupling, rims, precision=lax.Precision.HIGHEST, preferred_element_type=F32)


def shards(snapshots, mass_diag, lower_coupling, upper_coupling, band_offsets, start_basis):
    block_rows = snapshots.shape[0]
    rim_rows = lower_coupling.shape[1]
    total_rows = block_rows * lax.axis_size("rows")
    bottom_rim = snapshots[block_rows - rim_rows :, :]
    top_rim = snapshots[:rim_rows, :]
    below_one, below_two = (from_behind(bottom_rim, "rows", by) for by in (1, 2))
    above_one, above_two = (from_behind(top_rim, "rows", -by) for by in (1, 2))
    lower_rims = jnp.where(band_offsets[0, 0] == 1, below_one, below_two).astype(F32)
    upper_rims = jnp.where(band_offsets[0, 1] == 1, above_one, above_two).astype(F32)
    weighted = mass_diag[:, None] * snapshots.astype(F32)
    weighted = weighted.at[:rim_rows, :].add(rim_terms(lower_coupling[0], lower_rims))
    weighted = weighted.at[block_rows - rim_rows :, :].add(rim_terms(upper_coupling[0], upper_rims))
    weighted = weighted.astype(BF16)
    gathered = lax.all_gather(weighted, "groups", axis=1, tiled=True)
    gram_rows = lax.dot_general(weighted, gathered, (((0,), (0,)), ((), ())), preferred_element_type=F32)
    gram_rows = lax.psum(gram_rows, "rows") / total_rows
    gram = lax.all_gather(gram_rows, "groups", axis=0, tiled=True)
    group_index = lax.axis_index("groups")
    part_modes = start_basis.shape[1] // lax.axis_size("groups")
    high, low, start_ok = prepare_start(start_basis)
    basis_part, iterate_ok = iterate(group_index.reshape(1), part_modes, gram, high, low)
    basis_part = lax.cond(
        (start_ok[0] > 0) & (iterate_ok[0] > 0),
        lambda *_: basis_part,
        functools.partial(direct_part, group_index, part_modes),
        gram,
        start_basis,
    )
    return lax.dot_general(gathered, basis_part, (((1,), (1,)), ((), ())), preferred_element_type=F32)


def solution(mesh):
    placed = (
        P("rows", "groups"),
        P("rows"),
        P("rows", None, None),
        P("rows", None, None),
        P("rows", None),
        P(),
    )
    return jax.shard_map(
        shards, mesh=mesh, in_specs=placed, out_specs=P("rows", "groups"), check_vma=False
    )
```

time: 707 us -> 728 us (1.030)
  Pallas kernels: 0 us -> 40.6 us
  waiting for transfers between devices: 154 us -> 139 us
  loops' own time: 0.23 us -> 11.7 us
  matrix products: 95.6 us -> 87.1 us
    pallas_call x0 -> x2, Pallas kernels: none -> 40.6 us  [the longest x1 31.6 us: iterate(): pl.pallas_call(iterate_kernel, name='iterate', out_shape=(jax.ShapeDtypeS...]
    all_gather x1, waiting for transfers between devices: 34.2 us -> 22.6 us  [shards(): gram = lax.all_gather(gram_rows, 'groups', axis=0, tiled=True)]
    another operation x0 -> x1, loops' own time: none -> 11.5 us  [shards(): lax.cond((start_ok[0] > 0) & (iterate_ok[0] > 0), lambda *_: basis_part,...]
    another operation x21, matrix products: 37.5 us -> 26.9 us  [orthonormal(): lax.linalg.triangular_solve(lower, image, left_side=False, lower=True, tr...]
  transfers between devices with their start and end apart: 7 -> 7, of which waited for: 4 -> 4; matrix products, arithmetic and copies ran while one was open for 0% -> 1% of each run, Pallas kernels for 0% -> 1%
where the time goes in v1:
time: 728 us; the launch traced here: 724 us
  other arithmetic  369 us (51%)
  waiting for transfers between devices  139 us (19%)
  matrix products  87.1 us (12%)
  local copies, waits for them, and re-layouts  49.5 us (7%)
  Pallas kernels  40.6 us (6%)
  between operations  16 us (2%)
  loops' own time  11.7 us (2%)
  starting transfers between devices  11.2 us (2%)
    another operation x44, other arithmetic, orthonormal(): lower = jnp.linalg.cholesky(correlation)  238 us
    another operation x7, other arithmetic, orthonormal(): lax.linalg.triangular_solve(lower, image, left_side=False, lower=True, tr...  122 us
    psum x1, waiting for transfers between devices, shards(): gram_rows = lax.psum(gram_rows, 'rows') / total_rows  78 us
    all_gather x1, waiting for transfers between devices, shards(): gathered = lax.all_gather(weighted, 'groups', axis=1, tiled=True)  35.9 us
    another operation x40, local copies, waits for them, and re-layouts, orthonormal(): lax.linalg.triangular_solve(lower, image, left_side=False, lower=True, tr...  35.6 us
    pallas_call x1, Pallas kernels, iterate(): pl.pallas_call(iterate_kernel, name='iterate', out_shape=(jax.ShapeDtypeS...  31.6 us
    another operation x21, matrix products, orthonormal(): lax.linalg.triangular_solve(lower, image, left_side=False, lower=True, tr...  26.9 us
    dot_general x3, matrix products, direct_part(): jnp.dot(gram, basis, precision=lax.Precision.HIGHEST, preferred_element_t...  23.3 us
  transfers between devices with their start and end apart: 7, of which 4 were waited for; matrix products, arithmetic and copies ran while one was open for 1% of the time, Pallas kernels for 1%

profile of v1, /device:TPU:0, one launch (start us, length us, event | category | flops | bytes accessed | tf_op | source)
XLA Modules:
  0.0 723.9 jit_solution(11811542411379421219)
XLA Ops:
  26.4 35.9 %all-gather.3.cloned.1.call-done = bf16[2048,1024]{0,1:T(8,128)(2,1)} async-done(((bf16[2048,256]{0,1:T(8,128)(2,1)}), bf16[2048,1024]{0,1:T(8,128)(2,1)}) %all-gather.3.cloned.1.call-update) | async-done | bytes 4194320 | tf_op jit(solution)/shard_map/all_gather | solution.py:228
  67.4 78.0 %all-reduce.3.cloned.1.call-done = f32[256,1024]{1,0:T(8,128)} async-done(((f32[256,1024]{1,0:T(8,128)}), f32[256,1024]{1,0:T(8,128)}) %all-reduce.3.cloned.1.call-update) | async-done | bytes 1048592 | tf_op jit(solution)/shard_map/psum | solution.py:230
  159.4 22.6 %all-gather.5.cloned.1.call-done.gram_ref = f32[1024,1024]{1,0:T(8,128)} async-done(((f32[256,1024]{1,0:T(8,128)}), f32[1024,1024]{1,0:T(8,128)}) %all-gather.5.cloned.1.call-update) | async-done | bytes 4194320 | tf_op jit(solution)/shard_map/all_gather | solution.py:231
  182.0 31.6 %iterate.1 = (bf16[128,1024]{1,0:T(8,128)(2,1)}, s32[1]{0:T(128)}) custom-call(s32[1]{0:T(128)} %bitcast.46.part_ref, f32[1024,1024]{1,0:T(8,128)} %all-gather.5.cloned.1.call-done.gram_ref, bf16[512,1024]{1,0:T(8,128)(2,1)} %get-tuple-element.50.high_in, bf16[512,1024]{1,0:T(8,128)(2,1)} %get-tuple-element.51.low_in), custom_call_target="tpu_custom_call" | custom-call | flops 20132659200 | bytes 4194304 | tf_op jit(solution)/shard_map/iterate/pallas_call | solution.py:169
  214.2 498.5 %conditional.1 = (bf16[128,1024]{1,0:T(8,128)(2,1)}) conditional(s32[]{:T(128)} %bitcast.47, (f32[1024,1024]{1,0:T(8,128)S(1)}, f32[1024,512]{1,0:T(8,128)S(1)}, s32[]{:T(128)}) %tuple.107, bf16[128,1024]{1,0:T(8,128)(2,1)} %get-tuple-element.53), branch_computations={%region_1.12_spmd, %region_10.13_spmd} | conditional | flops 36253204480 | bytes 181416736 | solution.py:236
  234.6 11.9 %cholesky.374 = f32[128,128]{1,0:T(8,128)S(1)} custom-call(f32[128,128]{1,0:T(8,128)S(1)} %cholesky.586), custom_call_target="Cholesky" | custom-call | tf_op jit(solution)/shard_map/cond/branch_0_fun/jit(cholesky)/cholesky | solution.py:192
  246.5 9.8 %custom-call.31 = f32[1,128,128]{1,2,0:T(8,128)S(1)} custom-call(f32[1,128,128]{2,1,0:T(8,128)S(1)} %get-tuple-element.136), custom_call_target="InvertDiagBlocksLowerTriangular" | custom-call | tf_op jit(solution)/shard_map/cond/branch_0_fun/jit(cholesky)/cholesky | solution.py:192
  258.9 11.7 %cholesky.393 = f32[128,128]{1,0:T(8,128)S(1)} custom-call(f32[128,128]{1,0:T(8,128)S(1)} %cholesky.590), custom_call_target="Cholesky" | custom-call | tf_op jit(solution)/shard_map/cond/branch_0_fun/jit(cholesky)/cholesky | solution.py:192
  272.7 9.8 %custom-call.32 = f32[1,128,128]{1,2,0:T(8,128)S(1)} custom-call(f32[1,128,128]{2,1,0:T(8,128)S(1)} %get-tuple-element.133), custom_call_target="InvertDiagBlocksLowerTriangular" | custom-call | tf_op jit(solution)/shard_map/cond/branch_0_fun/jit(cholesky)/cholesky | solution.py:192
  284.1 11.9 %cholesky.414 = f32[128,128]{1,0:T(8,128)S(1)} custom-call(f32[128,128]{1,0:T(8,128)S(1)} %cholesky.595), custom_call_target="Cholesky" | custom-call | tf_op jit(solution)/shard_map/cond/branch_0_fun/jit(cholesky)/cholesky | solution.py:192
  297.4 9.8 %custom-call.33 = f32[1,128,128]{1,2,0:T(8,128)S(1)} custom-call(f32[1,128,128]{2,1,0:T(8,128)S(1)} %get-tuple-element.130), custom_call_target="InvertDiagBlocksLowerTriangular" | custom-call | tf_op jit(solution)/shard_map/cond/branch_0_fun/jit(cholesky)/cholesky | solution.py:192
  308.7 11.7 %cholesky.431 = f32[128,128]{1,0:T(8,128)S(1)} custom-call(f32[128,128]{1,0:T(8,128)S(1)} %convolution_subtract_fusion.14), custom_call_target="Cholesky" | custom-call | tf_op jit(solution)/shard_map/cond/branch_0_fun/jit(cholesky)/cholesky | solution.py:192
  322.9 11.9 %while.8 = (s32[]{:T(128)}, f32[512,512]{1,0:T(8,128)}, s32[4,2]{0,1:T(2,128)S(1)}, f32[4,128,128]{2,1,0:T(8,128)S(1)}, s32[]{:T(128)}) while((s32[]{:T(128)}, f32[512,512]{1,0:T(8,128)}, s32[4,2]{0,1:T(2,128)S(1)}, f32[4,128,128]{2,1,0:T(8,128)S(1)}, s32[]{:T(128)}) %tuple.89), condition=%wide.while_cond.2, body=%wide.while_body.2.sunk | while | flops 2 | bytes 131181 | solution.py:193
  334.8 39.7 %custom-call.34 = f32[4,128,128]{1,2,0:T(8,128)S(1)} custom-call(f32[4,128,128]{2,1,0:T(8,128)S(1)} %get-tuple-element.74), custom_call_target="InvertDiagBlocksLowerTriangular" | custom-call | tf_op jit(solution)/shard_map/cond/branch_0_fun/triangular_solve/custom-call.3 | solution.py:193
  400.1 11.7 %cholesky.446 = f32[128,128]{1,0:T(8,128)S(1)} custom-call(f32[128,128]{1,0:T(8,128)S(1)} %cholesky.599), custom_call_target="Cholesky" | custom-call | tf_op jit(solution)/shard_map/cond/branch_0_fun/jit(cholesky)/cholesky | solution.py:192
  412.0 10.0 %custom-call.35 = f32[1,128,128]{1,2,0:T(8,128)S(1)} custom-call(f32[1,128,128]{2,1,0:T(8,128)S(1)} %get-tuple-element.126), custom_call_target="InvertDiagBlocksLowerTriangular" | custom-call | tf_op jit(solution)/shard_map/cond/branch_0_fun/jit(cholesky)/cholesky | solution.py:192
  424.5 11.7 %cholesky.465 = f32[128,128]{1,0:T(8,128)S(1)} custom-call(f32[128,128]{1,0:T(8,128)S(1)} %cholesky.603), custom_call_target="Cholesky" | custom-call | tf_op jit(solution)/shard_map/cond/branch_0_fun/jit(cholesky)/cholesky | solution.py:192
  439.0 9.8 %custom-call.36 = f32[1,128,128]{1,2,0:T(8,128)S(1)} custom-call(f32[1,128,128]{2,1,0:T(8,128)S(1)} %get-tuple-element.123), custom_call_target="InvertDiagBlocksLowerTriangular" | custom-call | tf_op jit(solution)/shard_map/cond/branch_0_fun/jit(cholesky)/cholesky | solution.py:192
  450.3 12.0 %cholesky.486 = f32[128,128]{1,0:T(8,128)S(1)} custom-call(f32[128,128]{1,0:T(8,128)S(1)} %cholesky.608), custom_call_target="Cholesky" | custom-call | tf_op jit(solution)/shard_map/cond/branch_0_fun/jit(cholesky)/cholesky | solution.py:192
  463.8 9.8 %custom-call.37 = f32[1,128,128]{1,2,0:T(8,128)S(1)} custom-call(f32[1,128,128]{2,1,0:T(8,128)S(1)} %get-tuple-element.120), custom_call_target="InvertDiagBlocksLowerTriangular" | custom-call | tf_op jit(solution)/shard_map/cond/branch_0_fun/jit(cholesky)/cholesky | solution.py:192
  475.1 11.7 %cholesky.503 = f32[128,128]{1,0:T(8,128)S(1)} custom-call(f32[128,128]{1,0:T(8,128)S(1)} %convolution_subtract_fusion.13), custom_call_target="Cholesky" | custom-call | tf_op jit(solution)/shard_map/cond/branch_0_fun/jit(cholesky)/cholesky | solution.py:192
  489.2 11.9 %while.9 = (s32[]{:T(128)}, f32[512,512]{1,0:T(8,128)}, s32[4,2]{0,1:T(2,128)S(1)}, f32[4,128,128]{2,1,0:T(8,128)S(1)}, s32[]{:T(128)}) while((s32[]{:T(128)}, f32[512,512]{1,0:T(8,128)}, s32[4,2]{0,1:T(2,128)S(1)}, f32[4,128,128]{2,1,0:T(8,128)S(1)}, s32[]{:T(128)}) %tuple.108), condition=%wide.while_cond.2.clone, body=%wide.while_body.2.clone.sunk | while | flops 2 | bytes 131181 | solution.py:193
  501.2 39.5 %custom-call.38 = f32[4,128,128]{1,2,0:T(8,128)S(1)} custom-call(f32[4,128,128]{2,1,0:T(8,128)S(1)} %get-tuple-element.75), custom_call_target="InvertDiagBlocksLowerTriangular" | custom-call | tf_op jit(solution)/shard_map/cond/branch_0_fun/triangular_solve/custom-call.3 | solution.py:193
  563.1 11.7 %cholesky.518 = f32[128,128]{1,0:T(8,128)S(1)} custom-call(f32[128,128]{1,0:T(8,128)S(1)} %cholesky.612), custom_call_target="Cholesky" | custom-call | tf_op jit(solution)/shard_map/cond/branch_0_fun/jit(cholesky)/cholesky | solution.py:192
  575.0 9.8 %custom-call.39 = f32[1,128,128]{1,2,0:T(8,128)S(1)} custom-call(f32[1,128,128]{2,1,0:T(8,128)S(1)} %get-tuple-element.116), custom_call_target="InvertDiagBlocksLowerTriangular" | custom-call | tf_op jit(solution)/shard_map/cond/branch_0_fun/jit(cholesky)/cholesky | solution.py:192
  587.3 12.1 %cholesky.537 = f32[128,128]{1,0:T(8,128)S(1)} custom-call(f32[128,128]{1,0:T(8,128)S(1)} %cholesky.616), custom_call_target="Cholesky" | custom-call | tf_op jit(solution)/shard_map/cond/branch_0_fun/jit(cholesky)/cholesky | solution.py:192
  602.2 9.8 %custom-call.40 = f32[1,128,128]{1,2,0:T(8,128)S(1)} custom-call(f32[1,128,128]{2,1,0:T(8,128)S(1)} %get-tuple-element.113), custom_call_target="InvertDiagBlocksLowerTriangular" | custom-call | tf_op jit(solution)/shard_map/cond/branch_0_fun/jit(cholesky)/cholesky | solution.py:192
  613.6 11.7 %cholesky.558 = f32[128,128]{1,0:T(8,128)S(1)} custom-call(f32[128,128]{1,0:T(8,128)S(1)} %cholesky.621), custom_call_target="Cholesky" | custom-call | tf_op jit(solution)/shard_map/cond/branch_0_fun/jit(cholesky)/cholesky | solution.py:192
  626.7 9.8 %custom-call.41 = f32[1,128,128]{1,2,0:T(8,128)S(1)} custom-call(f32[1,128,128]{2,1,0:T(8,128)S(1)} %get-tuple-element.110), custom_call_target="InvertDiagBlocksLowerTriangular" | custom-call | tf_op jit(solution)/shard_map/cond/branch_0_fun/jit(cholesky)/cholesky | solution.py:192
  638.0 11.9 %cholesky.575 = f32[128,128]{1,0:T(8,128)S(1)} custom-call(f32[128,128]{1,0:T(8,128)S(1)} %convolution_subtract_fusion.12), custom_call_target="Cholesky" | custom-call | tf_op jit(solution)/shard_map/cond/branch_0_fun/jit(cholesky)/cholesky | solution.py:192
  652.3 11.9 %while.10 = (s32[]{:T(128)}, f32[512,512]{1,0:T(8,128)}, s32[4,2]{0,1:T(2,128)S(1)}, f32[4,128,128]{2,1,0:T(8,128)S(1)}, s32[]{:T(128)}) while((s32[]{:T(128)}, f32[512,512]{1,0:T(8,128)}, s32[4,2]{0,1:T(2,128)S(1)}, f32[4,128,128]{2,1,0:T(8,128)S(1)}, s32[]{:T(128)}) %tuple.109), condition=%wide.while_cond.2.clone.1, body=%wide.while_body.2.clone.1.sunk | while | flops 2 | bytes 131181 | solution.py:193
  664.2 39.3 %custom-call.42 = f32[4,128,128]{1,2,0:T(8,128)S(1)} custom-call(f32[4,128,128]{2,1,0:T(8,128)S(1)} %get-tuple-element.76), custom_call_target="InvertDiagBlocksLowerTriangular" | custom-call | tf_op jit(solution)/shard_map/cond/branch_0_fun/triangular_solve/custom-call.3 | solution.py:193
  (185 shorter events, 179.3 us)
Async XLA Ops:
  6.5 15.9 %copy-start = (f32[1,128,128]{2,1,0:T(8,128)S(1)}, f32[1,128,128]{2,1,0:T(8,128)}, u32[]{:S(2)}) copy-start(f32[1,128,128]{2,1,0:T(8,128)} %param.17) | copy-start | bytes 196612
  6.5 13.4 %copy-start.12 = (f32[2048]{0:T(1024)S(1)}, f32[2048]{0:T(1024)}, u32[]{:S(2)}) copy-start(f32[2048]{0:T(1024)} %param.16) | copy-start | bytes 24580
  6.5 55.8 %all-gather.3.cloned.1.call-start = ((), (), s32[]{:S(2)}) async-start(), calls=%async_computation | async-start | bytes 5242880 | tf_op jit(solution)/shard_map/all_gather | solution.py:228
  7.5 14.9 %collective-permute-start = (bf16[128,256]{1,0:T(8,128)(2,1)S(1)}, bf16[128,256]{1,0:T(8,128)(2,1)S(1)}, u32[]{:S(2)}, u32[]{:S(2)}) collective-permute-start(bf16[128,256]{1,0:T(8,128)(2,1)S(1)} %get-tuple-element.146), channel_id=1, source_target_pairs={{0,4},{4,8},{8,12},{12,16},{16,20},{20,24},{24,28},{1,5},{5,9},{9,... | collective-permute-start | bytes 196616 | tf_op jit(solution)/shard_map/ppermute | solution.py:207
  12.3 10.1 %collective-permute-start.1 = (bf16[128,256]{1,0:T(8,128)(2,1)S(1)}, bf16[128,256]{1,0:T(8,128)(2,1)S(1)}, u32[]{:S(2)}, u32[]{:S(2)}) collective-permute-start(bf16[128,256]{1,0:T(8,128)(2,1)S(1)} %get-tuple-element.146), channel_id=1, source_target_pairs={{0,8},{4,12},{8,16},{12,20},{16,24},{20,28},{1,9},{5,13},{9,17},{1... | collective-permute-start | bytes 196616 | tf_op jit(solution)/shard_map/ppermute | solution.py:207
  15.8 6.9 collective-permute-start.2
  17.1 7.7 %collective-permute-start.3 = (bf16[128,256]{1,0:T(8,128)(2,1)S(1)}, bf16[128,256]{1,0:T(8,128)(2,1)S(1)}, u32[]{:S(2)}, u32[]{:S(2)}) collective-permute-start(bf16[128,256]{1,0:T(8,128)(2,1)S(1)} %get-tuple-element.145), channel_id=1, source_target_pairs={{8,0},{12,4},{16,8},{20,12},{24,16},{28,20},{9,1},{13,5},{17,9},{2... | collective-permute-start | bytes 196616 | tf_op jit(solution)/shard_map/ppermute | solution.py:207
  19.9 0.7 copy-start.13
  20.0 4.9 copy-start.11
  26.3 119.1 %all-reduce.3.cloned.1.call-start = ((), (), s32[]{:S(2)}) async-start(), calls=%async_computation.1 | async-start | bytes 2097152 | tf_op jit(solution)/shard_map/psum | solution.py:230
  67.1 80.6 %copy-start.5 = (f32[1024,512]{1,0:T(8,128)S(1)}, f32[1024,512]{1,0:T(8,128)}, u32[]{:S(2)}) copy-start(f32[1024,512]{1,0:T(8,128)} %param.20) | copy-start | bytes 6291460
  67.1 114.8 %all-gather.5.cloned.1.call-start = ((), (), s32[]{:S(2)}) async-start(), calls=%async_computation.2 | async-start | bytes 5242880 | tf_op jit(solution)/shard_map/all_gather | solution.py:231
  182.0 32.2 %copy-start.1 = (f32[1024,1024]{1,0:T(8,128)S(1)}, f32[1024,1024]{1,0:T(8,128)}, u32[]{:S(2)}) copy-start(f32[1024,1024]{1,0:T(8,128)} %all-gather.5.cloned.1.call-done.gram_ref) | copy-start | bytes 12582916
  216.8 1.4 copy-start.6
  216.9 10.4 %copy-start.2 = (f32[1024,1024]{1,0:T(8,128)}, f32[1024,1024]{1,0:T(8,128)S(1)}, u32[]{:S(2)}) copy-start(f32[1024,1024]{1,0:T(8,128)S(1)} %get-tuple-element.41) | copy-start | bytes 12582916 | tf_op jit(solution)/shard_map/cond
  233.6 1.0 copy-start.8
  380.4 5.3 copy-start.3
  399.1 1.0 copy-start.9
  545.0 3.7 copy-start.4
  562.1 1.0 copy-start.10
  708.5 2.3 copy-start.7
Sparse Core Ops, SparseCore 0:
  26.5 35.7 all-gather.2
  67.3 78.1 all-reduce.2
  147.9 34.0 all-gather.4

commit v2 on v1

--- a/solution.py
+++ b/solution.py
@@ -82,18 +82,32 @@
 
 
 def iterate_kernel(
-    part_ref, gram_ref, high_in, low_in, basis_ref, ok_ref, gram_high, gram_low, image, high, low, corr_ref, x_ref, e_ref
+    second_rows, part_ref, gram_ref, high_in, low_in, basis_ref, ok_ref, gram_high, gram_low, image, high, low, corr_ref, x_ref, e_ref
 ):
     modes, snaps = image.shape
     tile = 256
     part_modes = basis_ref.shape[0]
 
-    def split_gram(step, carry):
-        rows = pl.ds(pl.multiple_of(step * tile, tile), tile)
-        gram_high[rows, :], gram_low[rows, :] = split(gram_ref[rows, :])
-        return carry
-
-    lax.fori_loop(0, snaps // tile, split_gram, 0)
+    width = gram_ref.shape[-1]
+    quarter, half = width // 4, width // 2
+    first = gram_ref.shape[3] - second_rows
+
+    def place(row, col, block):
+        rows, cols = block.shape
+        gram_high[row : row + rows, col : col + cols], gram_low[row : row + rows, col : col + cols] = split(block)
+
+    for x in range(2):
+        for c in range(2):
+            corner = (2 * x + c) * width
+            place(corner, corner, gram_ref[x, c, 0, : 3 * quarter, :])
+            place(corner + 3 * quarter, corner, gram_ref[x, c, 1, :quarter, :])
+            side = gram_ref[x, c, 1, quarter : 3 * quarter, :]
+            place(2 * x * width + c * half, (2 * x + 1) * width, side)
+            place((2 * x + 1) * width, 2 * x * width + c * half, side.T)
+            for y in range(2):
+                cross = gram_ref[x, c, y, first : first + half, :]
+                place(c * width + y * half, (2 + x) * width, cross)
+                place((2 + x) * width, c * width + y * half, cross.T)
     high[...] = high_in[...]
     low[...] = low_in[...]
     ok = jnp.bool_(True)
@@ -164,10 +178,10 @@
     )(start_basis.T)
 
 
-def iterate(part, part_modes, gram, high, low):
+def iterate(part, part_modes, second_rows, gram, high, low):
     modes, snaps = high.shape
     return pl.pallas_call(
-        iterate_kernel,
+        functools.partial(iterate_kernel, second_rows),
         name="iterate",
         out_shape=(jax.ShapeDtypeStruct((part_modes, snaps), BF16), jax.ShapeDtypeStruct((1,), jnp.int32)),
         in_specs=[SMEM, VMEM, VMEM, VMEM],
@@ -201,43 +215,280 @@
     return lax.dynamic_slice_in_dim(basis.astype(BF16).T, group_index * part_modes, part_modes, 0)
 
 
-def from_behind(value, axis, by):
-    devices = lax.axis_size(axis)
-    pairs = [(i, i + by) for i in range(devices) if 0 <= i + by < devices]
-    return lax.ppermute(value, axis, pairs)
+def dot_tn(a, b):
+    return lax.dot_general(a, b, (((0,), (0,)), ((), ())), preferred_element_type=F32)
 
 
 def rim_terms(coupling, rims):
-    return jnp.dot(coupling, rims, precision=lax.Precision.HIGHEST, preferred_element_type=F32)
+    high, rest = split(coupling)
+    middle = (coupling - high.astype(F32)).astype(BF16)
+    low = (coupling - high.astype(F32) - middle.astype(F32)).astype(BF16)
+    return dot_nn(high, rims) + (dot_nn(middle, rims) + dot_nn(low, rims))
+
+
+class Layout:
+    def __init__(self, devices, width):
+        self.depth = devices // 2
+        up = lambda rows: -(-rows // (8 * self.depth)) * 8
+        self.chunks = (up(width * 3 // 4), up(width // 2))
+        self.halves = tuple(chunk * self.depth for chunk in self.chunks)
+
+
+def exchange_kernel(
+    lay, base_ref, rims_ref, top_ref, bottom_ref, lower_ref, upper_ref, pick_ref, wall_out, gram_out,
+    wall, rims_in, part, cross, cross_in, y_in0, y_in1, h0, h1, z_in0, z_in1, pieces, send_sem, recv_sem, out_sem,
+):
+    devices, depth = lax.axis_size("rows"), lay.depth
+    me, group = lax.axis_index("rows"), lax.axis_index("groups")
+    z, y, x, c = me // 2, me % 2, group // 2, group % 2
+    block_rows, width = base_ref.shape
+    rim = top_ref.shape[0]
+    middle_rows, half_rows = block_rows - 2 * rim, block_rows // 2
+    core_peer, x_peer = (me, 2 * x + 1 - c), (me, 2 * (1 - x) + c)
+    y_peer = (2 * z + 1 - y, group)
+    z_peers = [(2 * lax.rem(z + d, depth) + y, group) for d in range(1, depth)]
+    rim_peers = [(lax.rem(me + d + devices, devices), group) for d in (1, 2, -1, -2)]
+    peers = [core_peer, x_peer, y_peer] + z_peers + rim_peers
+
+    started = []
+
+    def send(src, dst, peer):
+        k = len(started)
+        copy = pltpu.make_async_remote_copy(
+            src_ref=src, dst_ref=dst, send_sem=send_sem.at[k], recv_sem=recv_sem.at[k],
+            device_id=peer, device_id_type=pl.DeviceIdType.MESH,
+        )
+        copy.start()
+        started.append(copy)
+        return copy
+
+    def part_of(ref, row, rows, col=None):
+        rows = pl.ds(pl.multiple_of(row, 8), rows)
+        return ref.at[rows, :] if col is None else ref.at[rows, pl.ds(pl.multiple_of(col * width, width), width)]
+
+    barrier = pltpu.get_barrier_semaphore()
+    for peer in peers:
+        pl.semaphore_signal(barrier, inc=1, device_id=peer, device_id_type=pl.DeviceIdType.MESH)
+    pl.semaphore_wait(barrier, len(peers))
+
+    rim_copies = [
+        send(src, rims_in.at[k], peer)
+        for k, (src, peer) in enumerate(zip((bottom_ref, bottom_ref, top_ref, top_ref), rim_peers))
+    ]
+    there = 1 - x
+    inner = rim + there * (half_rows - rim)
+    outer = there * (block_rows - rim)
+    to_x = [send(part_of(base_ref, inner, half_rows - rim), part_of(wall, inner, half_rows - rim, group), x_peer)]
+    to_core = [send(part_of(base_ref, rim, middle_rows), part_of(wall, rim, middle_rows, group), core_peer)]
+    mine = pl.ds(pl.multiple_of(group * width, width), width)
+    wall[rim : block_rows - rim, mine] = base_ref[rim : block_rows - rim, :]
+    for copy in rim_copies:
+        copy.wait_recv()
+    below = rims_in[0].astype(F32) * pick_ref[0] + rims_in[1].astype(F32) * pick_ref[1]
+    above = rims_in[2].astype(F32) * pick_ref[2] + rims_in[3].astype(F32) * pick_ref[3]
+    wall[:rim, mine] = (rims_ref[:rim, :] + rim_terms(lower_ref[...], below.astype(BF16))).astype(BF16)
+    wall[block_rows - rim :, mine] = (rims_ref[rim:, :] + rim_terms(upper_ref[...], above.astype(BF16))).astype(BF16)
+    to_x.append(send(part_of(wall, outer, rim, group), part_of(wall, outer, rim, group), x_peer))
+    for row in (0, block_rows - rim):
+        to_core.append(send(part_of(wall, row, rim, group), part_of(wall, row, rim, group), core_peer))
+
+    quarter, half = width // 4, width // 2
+    first, second = lay.halves
+    if first + second > 5 * quarter:
+        part[...] = jnp.zeros_like(part)
+    own = wall[:, mine]
+    diagonal = dot_tn(own, own)
+    part[0, : 3 * quarter, :] = diagonal[: 3 * quarter, :]
+    part[1, :quarter, :] = diagonal[3 * quarter :, :]
+    for copy in to_core:
+        copy.wait_recv()
+    left = pl.ds(pl.multiple_of(2 * x * width + c * half, half), half)
+    right = pl.ds(pl.multiple_of((2 * x + 1) * width, width), width)
+    part[1, quarter : 3 * quarter, :] = dot_tn(wall[:, left], wall[:, right])
+
+    total_rows = block_rows * devices
+
+    def window(ref, k, row, rows):
+        return ref.at[k, pl.ds(pl.multiple_of(row, 8), rows), :]
+
+    def segment(k):
+        rows, chunk, start = lay.halves[k], lay.chunks[k], k * first
+        y_in, h, z_in = (y_in0, h0, z_in0) if k == 0 else (y_in1, h1, z_in1)
+
+        def piece(xs, cs, ys, row, count):
+            return pieces.at[xs, cs, ys, pl.ds(pl.multiple_of(start + row, 8), count), :]
+
+        def same(xs, ys, row, count, peer):
+            return send(piece(xs, c, ys, row, count), piece(xs, c, ys, row, count), peer)
+
+        copy = send(window(part, 1 - y, start, rows), y_in, y_peer)
+        yield
+        copy.wait_recv()
+        h[...] = part[y, start : start + rows, :] + y_in[...]
+        copies = []
+        for d in range(1, depth):
+            there = lax.rem(z + d, depth)
+            copies.append(send(part_of(h, there * chunk, chunk), z_in.at[d - 1], z_peers[d - 1]))
+        yield
+        for copy in copies:
+            copy.wait_recv()
+        own = h[pl.ds(pl.multiple_of(z * chunk, 8), chunk), :]
+        for d in range(1, depth):
+            own = own + z_in[d - 1]
+        pieces[x, c, y, pl.ds(pl.multiple_of(start + z * chunk, 8), chunk), :] = own / total_rows
+        copies = [same(x, y, z * chunk, chunk, peer) for peer in z_peers]
+        yield
+        for copy in copies:
+            copy.wait_recv()
+        from_y = same(x, y, 0, rows, y_peer)
+        last = [same(x, y, 0, rows, core_peer)]
+        yield
+        from_x = same(x, y, 0, rows, x_peer)
+        yield
+        from_y.wait_recv()
+        part_x = same(x, 1 - y, 0, rows // 2, x_peer)
+        last.append(same(x, 1 - y, 0, rows, core_peer))
+        from_x.wait_recv()
+        part_y = same(1 - x, y, rows // 2, rows // 2, y_peer)
+        last.append(same(1 - x, y, 0, rows, core_peer))
+        yield
+        part_x.wait_recv()
+        part_y.wait_recv()
+        last.append(same(1 - x, 1 - y, 0, rows, core_peer))
+        yield
+        for copy in last:
+            copy.wait_recv()
+        yield
+
+    chip = segment(0)
+    next(chip)
+    next(chip)
+    next(chip)
+    for copy in to_x:
+        copy.wait_recv()
+    here = x * half_rows
+    other = 2 * (1 - x) + c
+    relay = send(part_of(wall, here, half_rows, other), part_of(wall, here, half_rows, other), core_peer)
+    relay.wait_recv()
+    rows = pl.ds(pl.multiple_of(here, half_rows), half_rows)
+    factor = wall[rows, pl.ds(pl.multiple_of(c * width, width), width)]
+    for side in range(2):
+        cross[side] = dot_tn(factor, wall[rows, (2 + side) * width : (3 + side) * width])
+    to_cross = send(cross.at[1 - x], cross_in, x_peer)
+    next(chip)
+    to_cross.wait_recv()
+    total = cross[x] + cross_in[...]
+    part[0, first : first + half, :] = total[:half, :]
+    part[1, first : first + half, :] = total[half:, :]
+    across = segment(1)
+    next(across)
+    next(chip)
+    next(across)
+    next(chip)
+    rest = send(part_of(wall, here, half_rows, group), part_of(wall, here, half_rows, group), x_peer)
+    next(across)
+    next(chip)
+    next(across)
+    next(across)
+    next(chip)
+    next(across)
+    rest.wait_recv()
+    far = there * half_rows
+    relay = send(part_of(wall, far, half_rows, other), part_of(wall, far, half_rows, other), core_peer)
+    next(across)
+    relay.wait_recv()
+    wall_copy = pltpu.make_async_copy(wall, wall_out, out_sem.at[0])
+    wall_copy.start()
+    next(across)
+    gram_copy = pltpu.make_async_copy(pieces, gram_out, out_sem.at[1])
+    gram_copy.start()
+    for copy in started:
+        copy.wait_send()
+    wall_copy.wait()
+    gram_copy.wait()
+
+
+def exchange(lay, base, rims, top, bottom, lower, upper, pick):
+    block_rows, width = base.shape
+    rim = top.shape[0]
+    first, second = lay.halves
+    depth = lay.depth
+    copies = 13 + 2 * (9 + 2 * (depth - 1))
+    pieces = (2, 2, 2, first + second, width)
+    return pl.pallas_call(
+        functools.partial(exchange_kernel, lay),
+        name="exchange",
+        out_shape=(jax.ShapeDtypeStruct((block_rows, 4 * width), BF16), jax.ShapeDtypeStruct(pieces, F32)),
+        in_specs=[VMEM] * 6 + [SMEM],
+        out_specs=(pl.BlockSpec(memory_space=pl.ANY), pl.BlockSpec(memory_space=pl.ANY)),
+        scratch_shapes=[
+            pltpu.VMEM((block_rows, 4 * width), BF16),
+            pltpu.VMEM((4, rim, width), BF16),
+            pltpu.VMEM((2, first + second, width), F32),
+            pltpu.VMEM((2, width, width), F32),
+            pltpu.VMEM((width, width), F32),
+            pltpu.VMEM((first, width), F32),
+            pltpu.VMEM((second, width), F32),
+            pltpu.VMEM((first, width), F32),
+            pltpu.VMEM((second, width), F32),
+            pltpu.VMEM((depth - 1, lay.chunks[0], width), F32),
+            pltpu.VMEM((depth - 1, lay.chunks[1], width), F32),
+            pltpu.VMEM(pieces, F32),
+            pltpu.SemaphoreType.DMA((copies,)),
+            pltpu.SemaphoreType.DMA((copies,)),
+            pltpu.SemaphoreType.DMA((2,)),
+        ],
+        compiler_params=pltpu.CompilerParams(collective_id=0, has_side_effects=True, vmem_limit_bytes=LIMIT),
+        cost_estimate=pl.CostEstimate(flops=4 * block_rows * width * width, bytes_accessed=2**23, transcendentals=0),
+    )(base, rims, top, bottom, lower, upper, pick)
+
+
+def whole_gram(pieces, second_rows):
+    first = pieces.shape[3] - second_rows
+    width = pieces.shape[-1]
+    quarter, half = width // 4, width // 2
+    grid = [[None] * 4 for _ in range(4)]
+    for x in range(2):
+        one, two = (
+            (pieces[x, c, 1, quarter : 3 * quarter, :], pieces[x, c, :, first : first + half, :].reshape(width, width))
+            for c in range(2)
+        )
+        side = jnp.concatenate([one[0], two[0]])
+        grid[2 * x][2 * x + 1], grid[2 * x + 1][2 * x] = side, side.T
+        for c, (_, cross) in enumerate((one, two)):
+            grid[c][2 + x], grid[2 + x][c] = cross, cross.T
+            grid[2 * x + c][2 * x + c] = jnp.concatenate([pieces[x, c, 0, : 3 * quarter], pieces[x, c, 1, :quarter]])
+    return jnp.block(grid)
 
 
 def shards(snapshots, mass_diag, lower_coupling, upper_coupling, band_offsets, start_basis):
-    block_rows = snapshots.shape[0]
+    block_rows, width = snapshots.shape
     rim_rows = lower_coupling.shape[1]
-    total_rows = block_rows * lax.axis_size("rows")
-    bottom_rim = snapshots[block_rows - rim_rows :, :]
-    top_rim = snapshots[:rim_rows, :]
-    below_one, below_two = (from_behind(bottom_rim, "rows", by) for by in (1, 2))
-    above_one, above_two = (from_behind(top_rim, "rows", -by) for by in (1, 2))
-    lower_rims = jnp.where(band_offsets[0, 0] == 1, below_one, below_two).astype(F32)
-    upper_rims = jnp.where(band_offsets[0, 1] == 1, above_one, above_two).astype(F32)
-    weighted = mass_diag[:, None] * snapshots.astype(F32)
-    weighted = weighted.at[:rim_rows, :].add(rim_terms(lower_coupling[0], lower_rims))
-    weighted = weighted.at[block_rows - rim_rows :, :].add(rim_terms(upper_coupling[0], upper_rims))
-    weighted = weighted.astype(BF16)
-    gathered = lax.all_gather(weighted, "groups", axis=1, tiled=True)
-    gram_rows = lax.dot_general(weighted, gathered, (((0,), (0,)), ((), ())), preferred_element_type=F32)
-    gram_rows = lax.psum(gram_rows, "rows") / total_rows
-    gram = lax.all_gather(gram_rows, "groups", axis=0, tiled=True)
-    group_index = lax.axis_index("groups")
+    devices = lax.axis_size("rows")
+    lay = Layout(devices, width)
+    second_rows = lay.halves[1]
+    row_index, group_index = lax.axis_index("rows"), lax.axis_index("groups")
+    below, above = band_offsets[0, 0], band_offsets[0, 1]
+    pick = jnp.stack(
+        [(below == by) & (row_index - by >= 0) for by in (1, 2)] + [(above == by) & (row_index + by < devices) for by in (1, 2)]
+    ).astype(F32)
+    top, bottom = snapshots[:rim_rows, :], snapshots[block_rows - rim_rows :, :]
+    base = (mass_diag[:, None] * snapshots.astype(F32)).astype(BF16)
+    rims = jnp.concatenate(
+        [
+            mass_diag[:rim_rows, None] * top.astype(F32),
+            mass_diag[block_rows - rim_rows :, None] * bottom.astype(F32),
+        ]
+    )
+    gathered, pieces = exchange(lay, base, rims, top, bottom, lower_coupling[0], upper_coupling[0], pick)
     part_modes = start_basis.shape[1] // lax.axis_size("groups")
     high, low, start_ok = prepare_start(start_basis)
-    basis_part, iterate_ok = iterate(group_index.reshape(1), part_modes, gram, high, low)
+    basis_part, iterate_ok = iterate(group_index.reshape(1), part_modes, second_rows, pieces, high, low)
     basis_part = lax.cond(
         (start_ok[0] > 0) & (iterate_ok[0] > 0),
         lambda *_: basis_part,
-        functools.partial(direct_part, group_index, part_modes),
-        gram,
+        lambda pieces, start: direct_part(group_index, part_modes, whole_gram(pieces, second_rows), start),
+        pieces,
         start_basis,
     )
     return lax.dot_general(gathered, basis_part, (((1,), (1,)), ((), ())), preferred_element_type=F32)

time: 728 us -> 659 us (0.905); the launches traced: 724 us -> 648 us
  waiting for transfers between devices: 139 us -> 0 us
  Pallas kernels: 40.6 us -> 105 us
  local copies, waits for them, and re-layouts: 49.5 us -> 63.1 us
  other arithmetic: 369 us -> 381 us
  between operations: 16 us -> 4.56 us
  starting transfers between devices: 11.2 us -> 0 us
    psum x1 -> x0, waiting for transfers between devices: 78 us -> none  [shards(): gram_rows = lax.psum(gram_rows, 'rows') / total_rows]
    pallas_call x1 -> x2, Pallas kernels: 31.6 us -> 95.6 us  [the longest x1 65 us: exchange(): pl.pallas_call(functools.partial(exchange_kernel, lay), name='exchange',...]
    all_gather x2 -> x0, waiting for transfers between devices: 58.5 us -> none  [the longest x1 35.9 us: shards(): gathered = lax.all_gather(weighted, 'groups', axis=1, tiled=True)]
    ppermute x4 -> x0, starting transfers between devices: 10.9 us -> none  [from_behind(): return lax.ppermute(value, axis, pairs)]
    concatenate x0 -> x3, other arithmetic: none -> 10.8 us  [the longest x2 10 us: whole_gram(): return jnp.block(grid)]
    another operation x44 -> x45, other arithmetic: 238 us -> 238 us  [orthonormal(): lower = jnp.linalg.cholesky(correlation)]
  transfers between devices with their start and end apart: 7 -> 0, of which waited for: 4 -> 0; matrix products, arithmetic and copies ran while one was open for 1% -> 0% of each run, Pallas kernels for 1% -> 0%
where the time goes in v2:
time: 659 us; the launch traced here: 648 us
  other arithmetic  381 us (58%)
  Pallas kernels  105 us (16%)
  matrix products  85.2 us (13%)
  local copies, waits for them, and re-layouts  63.1 us (10%)
  loops' own time  8.7 us (1%)
    another operation x45, other arithmetic, orthonormal(): lower = jnp.linalg.cholesky(correlation)  238 us
    another operation x7, other arithmetic, orthonormal(): lax.linalg.triangular_solve(lower, image, left_side=False, lower=True, tr...  122 us
    pallas_call x1, Pallas kernels, exchange(): pl.pallas_call(functools.partial(exchange_kernel, lay), name='exchange',...  65 us
    another operation x40, local copies, waits for them, and re-layouts, orthonormal(): lax.linalg.triangular_solve(lower, image, left_side=False, lower=True, tr...  33.7 us
    another operation x21, matrix products, orthonormal(): lax.linalg.triangular_solve(lower, image, left_side=False, lower=True, tr...  33.1 us
    pallas_call x1, Pallas kernels, iterate(): pl.pallas_call(functools.partial(iterate_kernel, second_rows), name='iter...  30.6 us
    dot_general x3, matrix products, direct_part(): jnp.dot(gram, basis, precision=lax.Precision.HIGHEST, preferred_element_t...  20.8 us
    another operation x18, matrix products, orthonormal(): lower = jnp.linalg.cholesky(correlation)  16.4 us

profile of v2, /device:TPU:0, one launch (start us, length us, event | category | flops | bytes accessed | tf_op | source)
XLA Modules:
  0.0 647.6 jit_solution(1405768937941983000)
XLA Ops:
  11.2 65.0 %exchange.1 = (bf16[2048,1024]{1,0:T(8,128)(2,1)}, f32[2,2,2,320,256]{4,3,2,1,0:T(8,128)S(1)}) custom-call(bf16[2048,256]{1,0:T(8,128)(2,1)} %multiply_convert_fusion.base_ref, f32[256,256]{1,0:T(8,128)} %pad_maximum_fusion.1.rims_ref, bf16[128,256]{1,0:T(8,128)(2,1)} %get-tuple-element.140.top_ref, bf16[128,256]{1,0:T(8,128)(2,1)} %get-tuple-element.139.bottom_ref, ...), custom_call_target="tpu_custom_call" | custom-call | flops 536870912 | bytes 8388608 | tf_op jit(solution)/shard_map/exchange/pallas_call | solution.py:418
  79.1 9.1 %prepare_start.1 = (bf16[512,1024]{1,0:T(8,128)(2,1)}, bf16[512,1024]{1,0:T(8,128)(2,1)}, s32[1]{0:T(128)}) custom-call(f32[512,1024]{1,0:T(8,128)} %bitcast.227), custom_call_target="tpu_custom_call" | custom-call | flops 4026531840 | bytes 2097152 | tf_op jit(solution)/shard_map/prepare_start/pallas_call | solution.py:165
  88.1 30.6 %iterate.1 = (bf16[128,1024]{1,0:T(8,128)(2,1)}, s32[1]{0:T(128)}) custom-call(s32[1]{0:T(128)} %bitcast.70.part_ref, f32[2,2,2,320,256]{4,3,2,1,0:T(8,128)S(1)} %get-tuple-element.29.gram_ref, bf16[512,1024]{1,0:T(8,128)(2,1)} %get-tuple-element.30.high_in, bf16[512,1024]{1,0:T(8,128)(2,1)} %get-tuple-element.31.low_in), custom_call_target="tpu_custom_call" | custom-call | flops 20132659200 | bytes 4194304 | tf_op jit(solution)/shard_map/iterate/pallas_call | solution.py:183
  120.1 522.6 %conditional.1 = (bf16[128,1024]{1,0:T(8,128)(2,1)}) conditional(s32[]{:T(128)} %bitcast.71, (f32[2,2,2,320,256]{4,3,2,1,0:T(8,128)S(1)}, f32[1024,512]{1,0:T(8,128)}, s32[]{:T(128)}) %tuple.13, bf16[128,1024]{1,0:T(8,128)(2,1)} %get-tuple-element.33), branch_computations={%region_0.11_spmd, %region_9.12_spmd} | conditional | flops 36272209920 | bytes 213922688 | solution.py:487
  138.6 8.0 %maximum_maximum_fusion = f32[1024,1024]{1,0:T(8,128)S(1)} fusion(f32[64,256]{1,0:T(8,128)S(1)} %get-tuple-element.92, f32[192,256]{1,0:T(8,128)S(1)} %get-tuple-element.88, f32[256,256]{1,0:T(8,128)} %copy.13, f32[256,256]{1,0:T(8,128)S(1)} %bitcast.222, f32[256,256]{1,0:T(8,128)} %copy.12, f32[128,256]{1,0:T(8,128)} %copy-done.9, f32[128,256]{1,0:T(8,128)} %copy-done.10, ...), kind=kLoop, calls=%fused_computation.6 | loop fusion | flops 17825792 | bytes 8388608 | tf_op jit(solution)/shard_map/cond/branch_0_fun/jit(block)/concatenate | solution.py:461
  160.6 11.9 %cholesky.374 = f32[128,128]{1,0:T(8,128)S(1)} custom-call(f32[128,128]{1,0:T(8,128)S(1)} %cholesky.586), custom_call_target="Cholesky" | custom-call | tf_op jit(solution)/shard_map/cond/branch_0_fun/jit(cholesky)/cholesky | solution.py:206
  172.7 9.8 %custom-call.31 = f32[1,128,128]{1,2,0:T(8,128)S(1)} custom-call(f32[1,128,128]{2,1,0:T(8,128)S(1)} %get-tuple-element.130), custom_call_target="InvertDiagBlocksLowerTriangular" | custom-call | tf_op jit(solution)/shard_map/cond/branch_0_fun/jit(cholesky)/cholesky | solution.py:206
  185.1 11.7 %cholesky.393 = f32[128,128]{1,0:T(8,128)S(1)} custom-call(f32[128,128]{1,0:T(8,128)S(1)} %cholesky.590), custom_call_target="Cholesky" | custom-call | tf_op jit(solution)/shard_map/cond/branch_0_fun/jit(cholesky)/cholesky | solution.py:206
  199.2 9.8 %custom-call.32 = f32[1,128,128]{1,2,0:T(8,128)S(1)} custom-call(f32[1,128,128]{2,1,0:T(8,128)S(1)} %get-tuple-element.127), custom_call_target="InvertDiagBlocksLowerTriangular" | custom-call | tf_op jit(solution)/shard_map/cond/branch_0_fun/jit(cholesky)/cholesky | solution.py:206
  210.6 12.1 %cholesky.414 = f32[128,128]{1,0:T(8,128)S(1)} custom-call(f32[128,128]{1,0:T(8,128)S(1)} %cholesky.595), custom_call_target="Cholesky" | custom-call | tf_op jit(solution)/shard_map/cond/branch_0_fun/jit(cholesky)/cholesky | solution.py:206
  224.0 9.8 %custom-call.33 = f32[1,128,128]{1,2,0:T(8,128)S(1)} custom-call(f32[1,128,128]{2,1,0:T(8,128)S(1)} %get-tuple-element.124), custom_call_target="InvertDiagBlocksLowerTriangular" | custom-call | tf_op jit(solution)/shard_map/cond/branch_0_fun/jit(cholesky)/cholesky | solution.py:206
  235.3 11.7 %cholesky.431 = f32[128,128]{1,0:T(8,128)S(1)} custom-call(f32[128,128]{1,0:T(8,128)S(1)} %convolution_subtract_fusion.14), custom_call_target="Cholesky" | custom-call | tf_op jit(solution)/shard_map/cond/branch_0_fun/jit(cholesky)/cholesky | solution.py:206
  249.5 11.2 %while.6 = (s32[]{:T(128)}, f32[512,512]{1,0:T(8,128)}, s32[4,2]{0,1:T(2,128)S(1)}, f32[4,128,128]{2,1,0:T(8,128)S(1)}, s32[]{:T(128)}) while((s32[]{:T(128)}, f32[512,512]{1,0:T(8,128)}, s32[4,2]{0,1:T(2,128)S(1)}, f32[4,128,128]{2,1,0:T(8,128)S(1)}, s32[]{:T(128)}) %tuple.93), condition=%wide.while_cond, body=%wide.while_body.sunk | while | flops 2 | bytes 131181 | solution.py:207
  260.7 39.5 %custom-call.34 = f32[4,128,128]{1,2,0:T(8,128)S(1)} custom-call(f32[4,128,128]{2,1,0:T(8,128)S(1)} %get-tuple-element.54), custom_call_target="InvertDiagBlocksLowerTriangular" | custom-call | tf_op jit(solution)/shard_map/cond/branch_0_fun/triangular_solve/custom-call.3 | solution.py:207
  325.5 11.7 %cholesky.446 = f32[128,128]{1,0:T(8,128)S(1)} custom-call(f32[128,128]{1,0:T(8,128)S(1)} %cholesky.599), custom_call_target="Cholesky" | custom-call | tf_op jit(solution)/shard_map/cond/branch_0_fun/jit(cholesky)/cholesky | solution.py:206
  337.4 10.2 %custom-call.35 = f32[1,128,128]{1,2,0:T(8,128)S(1)} custom-call(f32[1,128,128]{2,1,0:T(8,128)S(1)} %get-tuple-element.120), custom_call_target="InvertDiagBlocksLowerTriangular" | custom-call | tf_op jit(solution)/shard_map/cond/branch_0_fun/jit(cholesky)/cholesky | solution.py:206
  350.1 11.7 %cholesky.465 = f32[128,128]{1,0:T(8,128)S(1)} custom-call(f32[128,128]{1,0:T(8,128)S(1)} %cholesky.603), custom_call_target="Cholesky" | custom-call | tf_op jit(solution)/shard_map/cond/branch_0_fun/jit(cholesky)/cholesky | solution.py:206
  364.3 9.8 %custom-call.36 = f32[1,128,128]{1,2,0:T(8,128)S(1)} custom-call(f32[1,128,128]{2,1,0:T(8,128)S(1)} %get-tuple-element.117), custom_call_target="InvertDiagBlocksLowerTriangular" | custom-call | tf_op jit(solution)/shard_map/cond/branch_0_fun/jit(cholesky)/cholesky | solution.py:206
  375.7 11.7 %cholesky.486 = f32[128,128]{1,0:T(8,128)S(1)} custom-call(f32[128,128]{1,0:T(8,128)S(1)} %cholesky.608), custom_call_target="Cholesky" | custom-call | tf_op jit(solution)/shard_map/cond/branch_0_fun/jit(cholesky)/cholesky | solution.py:206
  388.9 9.8 %custom-call.37 = f32[1,128,128]{1,2,0:T(8,128)S(1)} custom-call(f32[1,128,128]{2,1,0:T(8,128)S(1)} %get-tuple-element.114), custom_call_target="InvertDiagBlocksLowerTriangular" | custom-call | tf_op jit(solution)/shard_map/cond/branch_0_fun/jit(cholesky)/cholesky | solution.py:206
  400.1 11.7 %cholesky.503 = f32[128,128]{1,0:T(8,128)S(1)} custom-call(f32[128,128]{1,0:T(8,128)S(1)} %convolution_subtract_fusion.13), custom_call_target="Cholesky" | custom-call | tf_op jit(solution)/shard_map/cond/branch_0_fun/jit(cholesky)/cholesky | solution.py:206
  414.3 11.2 %while.7 = (s32[]{:T(128)}, f32[512,512]{1,0:T(8,128)}, s32[4,2]{0,1:T(2,128)S(1)}, f32[4,128,128]{2,1,0:T(8,128)S(1)}, s32[]{:T(128)}) while((s32[]{:T(128)}, f32[512,512]{1,0:T(8,128)}, s32[4,2]{0,1:T(2,128)S(1)}, f32[4,128,128]{2,1,0:T(8,128)S(1)}, s32[]{:T(128)}) %tuple.104), condition=%wide.while_cond.clone, body=%wide.while_body.clone.sunk | while | flops 2 | bytes 131181 | solution.py:207
  425.5 39.5 %custom-call.38 = f32[4,128,128]{1,2,0:T(8,128)S(1)} custom-call(f32[4,128,128]{2,1,0:T(8,128)S(1)} %get-tuple-element.55), custom_call_target="InvertDiagBlocksLowerTriangular" | custom-call | tf_op jit(solution)/shard_map/cond/branch_0_fun/triangular_solve/custom-call.3 | solution.py:207
  490.6 11.7 %cholesky.518 = f32[128,128]{1,0:T(8,128)S(1)} custom-call(f32[128,128]{1,0:T(8,128)S(1)} %cholesky.612), custom_call_target="Cholesky" | custom-call | tf_op jit(solution)/shard_map/cond/branch_0_fun/jit(cholesky)/cholesky | solution.py:206
  502.5 9.9 %custom-call.39 = f32[1,128,128]{1,2,0:T(8,128)S(1)} custom-call(f32[1,128,128]{2,1,0:T(8,128)S(1)} %get-tuple-element.110), custom_call_target="InvertDiagBlocksLowerTriangular" | custom-call | tf_op jit(solution)/shard_map/cond/branch_0_fun/jit(cholesky)/cholesky | solution.py:206
  514.9 11.7 %cholesky.537 = f32[128,128]{1,0:T(8,128)S(1)} custom-call(f32[128,128]{1,0:T(8,128)S(1)} %cholesky.616), custom_call_target="Cholesky" | custom-call | tf_op jit(solution)/shard_map/cond/branch_0_fun/jit(cholesky)/cholesky | solution.py:206
  529.3 9.8 %custom-call.40 = f32[1,128,128]{1,2,0:T(8,128)S(1)} custom-call(f32[1,128,128]{2,1,0:T(8,128)S(1)} %get-tuple-element.107), custom_call_target="InvertDiagBlocksLowerTriangular" | custom-call | tf_op jit(solution)/shard_map/cond/branch_0_fun/jit(cholesky)/cholesky | solution.py:206
  540.7 11.7 %cholesky.558 = f32[128,128]{1,0:T(8,128)S(1)} custom-call(f32[128,128]{1,0:T(8,128)S(1)} %cholesky.621), custom_call_target="Cholesky" | custom-call | tf_op jit(solution)/shard_map/cond/branch_0_fun/jit(cholesky)/cholesky | solution.py:206
  553.9 9.8 %custom-call.41 = f32[1,128,128]{1,2,0:T(8,128)S(1)} custom-call(f32[1,128,128]{2,1,0:T(8,128)S(1)} %get-tuple-element.104), custom_call_target="InvertDiagBlocksLowerTriangular" | custom-call | tf_op jit(solution)/shard_map/cond/branch_0_fun/jit(cholesky)/cholesky | solution.py:206
  565.2 11.7 %cholesky.575 = f32[128,128]{1,0:T(8,128)S(1)} custom-call(f32[128,128]{1,0:T(8,128)S(1)} %convolution_subtract_fusion.12), custom_call_target="Cholesky" | custom-call | tf_op jit(solution)/shard_map/cond/branch_0_fun/jit(cholesky)/cholesky | solution.py:206
  579.3 11.5 %while.8 = (s32[]{:T(128)}, f32[512,512]{1,0:T(8,128)}, s32[4,2]{0,1:T(2,128)S(1)}, f32[4,128,128]{2,1,0:T(8,128)S(1)}, s32[]{:T(128)}) while((s32[]{:T(128)}, f32[512,512]{1,0:T(8,128)}, s32[4,2]{0,1:T(2,128)S(1)}, f32[4,128,128]{2,1,0:T(8,128)S(1)}, s32[]{:T(128)}) %tuple.105), condition=%wide.while_cond.clone.1, body=%wide.while_body.clone.1.sunk | while | flops 2 | bytes 131181 | solution.py:207
  590.9 39.6 %custom-call.42 = f32[4,128,128]{1,2,0:T(8,128)S(1)} custom-call(f32[4,128,128]{2,1,0:T(8,128)S(1)} %get-tuple-element.56), custom_call_target="InvertDiagBlocksLowerTriangular" | custom-call | tf_op jit(solution)/shard_map/cond/branch_0_fun/triangular_solve/custom-call.3 | solution.py:207
  (180 shorter events, 173.2 us)
Async XLA Ops:
  120.1 1.8 copy-start.9
  120.1 1.8 copy-start.10
  120.2 2.9 copy-start.11
  137.4 1.2 copy-start.5
  138.6 8.0 %copy-start.3 = (f32[1024,512]{1,0:T(8,128)S(1)}, f32[1024,512]{1,0:T(8,128)}, u32[]{:S(2)}) copy-start(f32[1024,512]{1,0:T(8,128)} %get-tuple-element.18) | copy-start | bytes 6291460 | tf_op jit(solution)/shard_map/cond
  146.7 6.7 %copy-start = (f32[1024,1024]{1,0:T(8,128)}, f32[1024,1024]{1,0:T(8,128)S(1)}, u32[]{:S(2)}) copy-start(f32[1024,1024]{1,0:T(8,128)S(1)} %maximum_maximum_fusion) | copy-start | bytes 12582916 | tf_op jit(solution)/shard_map/cond
  159.7 1.0 copy-start.6
  306.0 5.3 copy-start.1
  324.6 1.0 copy-start.7
  470.9 5.3 copy-start.2
  489.6 1.0 copy-start.8
  636.9 3.8 copy-start.4
